TPU v7x, 128 devices: a whole 4x4x4 slice. The times are simulated.
128 devices in a mesh: dp: 8 (over z, x_hi), seq: 16 (over y, x_lo, core).
Axes of the slice: x: 4 (x_hi: 2, x_lo: 2; x = x_hi * 2 + x_lo), y: 4, z: 4, core: 2. Of those that a mesh axis runs over, the one named last changes fastest.
Arguments:
- query_in: bfloat16 [8, 4096, 2048], P('dp', 'seq'), may hold values from -64 to 64
- key_in: bfloat16 [8, 4096, 2048], P('dp', 'seq'), may hold values from -4 to 4
- value_in: bfloat16 [8, 4096, 2048], P('dp', 'seq'), may hold values from -6 to 6
- out_grad: bfloat16 [8, 4096, 2048], P('dp', 'seq'), may hold values from -12 to 12
- out_weight: bfloat16 [2048, 2048], replicated, may hold values from -0.125 to 0.125
Outputs:
- query_grad: bfloat16 [8, 4096, 2048], P('dp', 'seq')
- key_grad: bfloat16 [8, 4096, 2048], P('dp', 'seq')
- value_grad: bfloat16 [8, 4096, 2048], P('dp', 'seq')
- weight_grad: float32 [2048, 2048], P('seq')
All inputs are finite; a program needn't handle non-finite values.
Results may differ from a plain program's by a relative error of at most 0.027.
Values may be sent and summed in bfloat16 or wider, within the bound.
A program may use at most 128 MiB of HBM per device.

v0:
```python
import math

import jax
import jax.numpy as jnp
from jax import lax
from jax.sharding import PartitionSpec as P

HEAD = 128


def shifted(block, axis, distance):
    devices = range(lax.axis_size(axis))
    route = [(i - distance, i) for i in devices if i - distance in devices]
    return lax.ppermute(block, axis, route)


def attend_head(query_head, key_head, value_head, keep_mask, grad_head, scaling):
    scores = jnp.dot(query_head, key_head.T, preferred_element_type=jnp.float32) * scaling
    scores = jnp.where(keep_mask, scores, -1e30)
    top_score = jnp.max(scores, axis=1, keepdims=True)
    exponent = jnp.where(keep_mask, jnp.exp(scores - top_score), 0.0)
    weights_full = exponent / jnp.sum(exponent, axis=1, keepdims=True)
    weights_low = weights_full.astype(jnp.bfloat16)
    attended = jnp.dot(weights_low, value_head, preferred_element_type=jnp.float32).astype(
        jnp.bfloat16
    )
    grad_weights = jnp.dot(grad_head, value_head.T, preferred_element_type=jnp.float32)
    inner_sum = jnp.sum(weights_full * grad_weights, axis=1, keepdims=True)
    grad_scores = (weights_full * (grad_weights - inner_sum) * scaling).astype(jnp.bfloat16)
    grad_query = jnp.dot(grad_scores, key_head, preferred_element_type=jnp.float32)
    grad_key = jnp.dot(grad_scores.T, query_head, preferred_element_type=jnp.float32)
    grad_value = jnp.dot(weights_low.T, grad_head, preferred_element_type=jnp.float32)
    return (attended, grad_query, grad_key, grad_value)


def split_rows(joined, amounts):
    pieces = []
    offset = 0
    for amount in amounts:
        pieces.append(joined[:, offset : offset + amount])
        offset = offset + amount
    return pieces


def per_device(query_in, key_in, value_in, out_grad, out_weight):
    tok_rows = query_in.shape[1]
    width = query_in.shape[2]
    heads = width // HEAD
    scaling = 1.0 / math.sqrt(HEAD)
    levels = lax.axis_size("seq").bit_length() - 1
    strides = [2**level for level in range(levels)]
    amounts = [tok_rows // stride for stride in strides]
    place = lax.axis_index("seq")
    queries = query_in[0]
    key_block = key_in[0]
    value_block = value_in[0]
    grad_out = out_grad[0]
    grad_attn = jnp.dot(grad_out, out_weight.T, preferred_element_type=jnp.float32).astype(
        jnp.bfloat16
    )
    paired = jnp.stack([key_block, value_block])
    samples = [paired[:, ::stride] for stride in strides]
    arrived = [shifted(samples[level], "seq", strides[level]) for level in range(levels)]
    key_all = jnp.concatenate([key_block] + [piece[0] for piece in arrived], axis=0)
    value_all = jnp.concatenate([value_block] + [piece[1] for piece in arrived], axis=0)
    causal = jnp.tril(jnp.ones((tok_rows, tok_rows), dtype=bool))
    keep_mask = jnp.concatenate(
        [causal]
        + [jnp.broadcast_to(place >= stride, (tok_rows, tok_rows // stride)) for stride in strides],
        axis=1,
    )

    def one_head(head_index):
        start = head_index * HEAD

        def pick(whole):
            return lax.dynamic_slice_in_dim(whole, start, HEAD, 1)

        return attend_head(
            pick(queries), pick(key_all), pick(value_all), keep_mask, pick(grad_attn), scaling
        )

    attended, grad_query, grad_key, grad_value = lax.map(one_head, jnp.arange(heads))

    def join_heads(stacked):
        return jnp.moveaxis(stacked, 0, 1).reshape(stacked.shape[1], width)

    grad_pairs = jnp.stack([join_heads(grad_key), join_heads(grad_value)])
    outgoing = [
        piece.astype(jnp.bfloat16) for piece in split_rows(grad_pairs[:, tok_rows:], amounts)
    ]
    total = grad_pairs[:, :tok_rows]
    returned = [shifted(outgoing[level], "seq", -strides[level]) for level in range(levels)]
    for level in range(levels):
        stride = strides[level]
        total = (
            total.reshape(2, amounts[level], stride, width)
            .at[:, :, 0]
            .add(returned[level].astype(jnp.float32))
            .reshape(2, tok_rows, width)
        )
    attended_rows = join_heads(attended)
    partial_sum = lax.psum_scatter(
        lax.dot_general(
            attended_rows, grad_out, (((0,), (0,)), ((), ())), preferred_element_type=jnp.float32
        ).astype(jnp.bfloat16),
        "seq",
        scatter_dimension=0,
        tiled=True,
    )
    weight_grad = lax.psum(partial_sum, "dp").astype(jnp.float32)
    query_grad = join_heads(grad_query).astype(jnp.bfloat16)[None]
    key_grad = total[0].astype(jnp.bfloat16)[None]
    value_grad = total[1].astype(jnp.bfloat16)[None]
    return (query_grad, key_grad, value_grad, weight_grad)


def solution(mesh):
    return jax.shard_map(
        per_device,
        mesh=mesh,
        in_specs=(
            P("dp", "seq", None),
            P("dp", "seq", None),
            P("dp", "seq", None),
            P("dp", "seq", None),
            P(),
        ),
        out_specs=(
            P("dp", "seq", None),
            P("dp", "seq", None),
            P("dp", "seq", None),
            P("seq", None),
        ),
        check_vma=False,
    )
```

profile of v0, /device:TPU:26, one launch (start us, length us, event | category | flops | bytes accessed | tf_op | source)
XLA Modules:
  0.0 515.0 jit_solution(2304102693886352570)
XLA Ops:
  9.9 1.9 collective-permute-start
  14.8 3.1 slice.175
  19.3 5.6 %slice.173 = bf16[2,128,2048]{2,1,0:T(8,128)(2,1)} slice(bf16[2,256,2048]{2,1,0:T(8,128)(2,1)S(1)} %constant_dynamic-update-slice_fusion.1), slice={[0:2:1], [0:256:2], [0:2048:1]} | slice | bytes 2097152 | tf_op jit(solution)/shard_map/slice | solution.py:62
  26.5 6.9 %convolution_convert_fusion.2 = bf16[256,2048]{1,0:T(8,128)(2,1)} fusion(bf16[2048,2048]{1,0:T(8,128)(2,1)} %param.19, bf16[1,256,2048]{2,1,0:T(8,128)(2,1)S(1)} %copy-done), kind=kOutput, calls=%fused_computation.35 | convolution fusion | flops 2148007936 | bytes 10485760 | tf_op jit(solution)/shard_map/dot_general | solution.py:58
  33.5 10.5 %collective-permute-done = bf16[2,256,2048]{2,1,0:T(8,128)(2,1)} collective-permute-done((bf16[2,256,2048]{2,1,0:T(8,128)(2,1)S(1)}, bf16[2,256,2048]{2,1,0:T(8,128)(2,1)}, u32[]{:S(2)}, u32[]{:S(2)}) %collective-permute-start) | collective-permute-done | bytes 2097184 | tf_op jit(solution)/shard_map/ppermute | solution.py:14
  45.8 7.4 %collective-permute-done.1 = bf16[2,128,2048]{2,1,0:T(8,128)(2,1)} collective-permute-done((bf16[2,128,2048]{2,1,0:T(8,128)(2,1)}, bf16[2,128,2048]{2,1,0:T(8,128)(2,1)}, u32[]{:S(2)}, u32[]{:S(2)}) %collective-permute-start.1) | collective-permute-done | bytes 1048608 | tf_op jit(solution)/shard_map/ppermute | solution.py:14
  59.1 182.4 %while.20 = (s32[]{:T(128)}, bf16[16,256,128]{1,2,0:T(8,128)(2,1)S(1)}, bf16[16,256,128]{2,1,0:T(8,128)(2,1)}, f32[16,736,128]{2,1,0:T(8,128)}, f32[16,736,128]{...) while((s32[]{:T(128)}, ...), condition=%wide.region_4.5_spmd, body=%wide.region_0.4_spmd.sunk | while | flops 294337792 | bytes 10534127 | solution.py:83
  123.6 2.0 fusion.70
  135.1 1.9 fusion.70
  146.5 2.0 fusion.70
  169.4 1.9 fusion.70
  192.2 1.9 fusion.70
  203.6 1.9 fusion.70
  241.5 5.6 %convolution_convert_fusion.1 = bf16[2048,2048]{1,0:T(8,128)(2,1)} fusion(bf16[256,2048]{0,1:T(8,128)(2,1)S(1)} %bitcast.111, bf16[1,256,2048]{2,1,0:T(8,128)(2,1)S(1)} %copy-done), kind=kOutput, calls=%fused_computation.33 | convolution fusion | flops 2151677952 | bytes 10485760 | tf_op jit(solution)/shard_map/dot_general | solution.py:104
  247.3 8.8 %copy.23 = f32[736,16,128]{2,1,0:T(8,128)} copy(f32[736,16,128]{2,0,1:T(8,128)} %bitcast.109) | data formatting | bytes 12058624 | tf_op jit(solution)/shard_map/transpose | solution.py:86
  256.1 7.1 %stack_reshape.7 = f32[1,736,2048]{2,1,0:T(8,128)} reshape(f32[736,16,128]{2,1,0:T(8,128)} %copy.23) | data formatting | bytes 12058624 | tf_op jit(solution)/shard_map/stack;reshape | solution.py:88
  263.2 8.8 %copy.22 = f32[736,16,128]{2,1,0:T(8,128)} copy(f32[736,16,128]{2,0,1:T(8,128)} %bitcast.110) | data formatting | bytes 12058624 | tf_op jit(solution)/shard_map/transpose | solution.py:86
  272.0 7.1 %stack_reshape.6 = f32[1,736,2048]{2,1,0:T(8,128)} reshape(f32[736,16,128]{2,1,0:T(8,128)} %copy.22) | data formatting | bytes 12058624 | tf_op jit(solution)/shard_map/stack;reshape | solution.py:88
  279.1 6.6 %constant_dynamic-update-slice_fusion.6 = f32[2,736,2048]{2,1,0:T(8,128)} fusion(f32[1,736,2048]{2,1,0:T(8,128)} %stack_reshape.6), kind=kLoop, calls=%fused_computation.74 | loop fusion | bytes 12058624
  285.7 3.0 constant_dynamic-update-slice_fusion.5
  288.7 5.5 %convert.19 = bf16[2,736,2048]{2,1,0:T(8,128)(2,1)S(1)} convert(f32[2,736,2048]{2,1,0:T(8,128)} %constant_dynamic-update-slice_fusion.5) | non-fusion elementwise | flops 3014656 | bytes 18087936 | tf_op jit(solution)/shard_map/convert.8
  295.7 19.5 %collective-permute-start.4 = (bf16[2,256,2048]{2,1,0:T(8,128)(2,1)}, bf16[2,256,2048]{2,1,0:T(8,128)(2,1)}, u32[]{:S(2)}, u32[]{:S(2)}) collective-permute-start(bf16[2,256,2048]{2,1,0:T(8,128)(2,1)} %slice.202), channel_id=1, source_target_pairs={{1,0},{2,1},{3,2},{4,3},{5,4},{6,5},{7,6},{8,7},{9,8},{10,9},{11,1... | collective-permute-start | bytes 6291464 | tf_op jit(solution)/shard_map/ppermute | solution.py:14
  316.3 2.2 collective-permute-start.5
  322.0 8.7 %collective-permute-start.7 = (bf16[2,32,2048]{2,1,0:T(8,128)(2,1)S(1)}, bf16[2,32,2048]{2,1,0:T(8,128)(2,1)S(1)}, u32[]{:S(2)}, u32[]{:S(2)}) collective-permute-start(bf16[2,32,2048]{2,1,0:T(8,128)(2,1)S(1)} %copy-done.9), channel_id=1, source_target_pairs={{8,0},{9,1},{10,2},{11,3},{12,4},{13,5},{14,6},{15,7},{24,16},{25,... | collective-permute-start | bytes 786440 | tf_op jit(solution)/shard_map/ppermute | solution.py:14
  332.4 63.1 %collective-permute-done.4 = bf16[2,256,2048]{2,1,0:T(8,128)(2,1)} collective-permute-done((bf16[2,256,2048]{2,1,0:T(8,128)(2,1)}, bf16[2,256,2048]{2,1,0:T(8,128)(2,1)}, u32[]{:S(2)}, u32[]{:S(2)}) %collective-permute-start.4) | collective-permute-done | bytes 2097184 | tf_op jit(solution)/shard_map/ppermute | solution.py:14
  395.4 3.5 slice_add_fusion
  398.9 3.2 copy.24
  402.4 7.9 %collective-permute-done.5 = bf16[2,128,2048]{2,1,0:T(8,128)(2,1)S(1)} collective-permute-done((bf16[2,128,2048]{2,1,0:T(8,128)(2,1)}, bf16[2,128,2048]{2,1,0:T(8,128)(2,1)S(1)}, u32[]{:S(2)}, u32[]{:S(2)}) %collective-permute-start.5) | collective-permute-done | bytes 1048608 | tf_op jit(solution)/shard_map/ppermute | solution.py:14
  415.8 2.1 convert.23
  417.9 3.8 fusion.38
  424.9 81.2 %all-reduce.2.cloned.1.call-done = bf16[128,2048]{1,0:T(8,128)(2,1)} async-done(((bf16[128,2048]{1,0:T(8,128)(2,1)}), bf16[128,2048]{1,0:T(8,128)(2,1)}) %all-reduce.2.cloned.1.call-update) | async-done | bytes 524304 | tf_op jit(solution)/shard_map/psum | solution.py:111
  506.1 2.1 convert_element_type.74
  (244 shorter events, 192.7 us)
Async XLA Ops:
  7.2 19.3 %copy-start = (bf16[1,256,2048]{2,1,0:T(8,128)(2,1)S(1)}, bf16[1,256,2048]{2,1,0:T(8,128)(2,1)}, u32[]{:S(2)}) copy-start(bf16[1,256,2048]{2,1,0:T(8,128)(2,1)} %param.18) | copy-start | bytes 3145732
  7.2 410.7 %reduce-scatter.2.cloned.1.call-start = ((), (), s32[]{:S(2)}) async-start(), calls=%async_computation.1 | async-start | bytes 8912896 | tf_op jit(solution)/shard_map/reduce_scatter | solution.py:103
  9.9 34.1 %collective-permute-start = (bf16[2,256,2048]{2,1,0:T(8,128)(2,1)S(1)}, bf16[2,256,2048]{2,1,0:T(8,128)(2,1)}, u32[]{:S(2)}, u32[]{:S(2)}) collective-permute-start(bf16[2,256,2048]{2,1,0:T(8,128)(2,1)S(1)} %constant_dynamic-update-slice_fusion.1), channel_id=1, source_target_pairs={{0,1},{1,2},{2,3},{3,4},{4,5},{5,6},{6,7},{7,8},{8,9},{9,10},{10,1... | collective-permute-start | bytes 6291464 | tf_op jit(solution)/shard_map/ppermute | solution.py:14
  13.6 42.0 %collective-permute-start.3 = (bf16[2,32,2048]{2,1,0:T(8,128)(2,1)}, bf16[2,32,2048]{2,1,0:T(8,128)(2,1)}, u32[]{:S(2)}, u32[]{:S(2)}) collective-permute-start(bf16[2,32,2048]{2,1,0:T(8,128)(2,1)} %slice.177), channel_id=1, source_target_pairs={{0,8},{1,9},{2,10},{3,11},{4,12},{5,13},{6,14},{7,15},{16,24},{17,... | collective-permute-start | bytes 786440 | tf_op jit(solution)/shard_map/ppermute | solution.py:14
  18.0 36.5 %collective-permute-start.2 = (bf16[2,64,2048]{2,1,0:T(8,128)(2,1)}, bf16[2,64,2048]{2,1,0:T(8,128)(2,1)}, u32[]{:S(2)}, u32[]{:S(2)}) collective-permute-start(bf16[2,64,2048]{2,1,0:T(8,128)(2,1)} %slice.175), channel_id=1, source_target_pairs={{0,4},{1,5},{2,6},{3,7},{4,8},{5,9},{6,10},{7,11},{8,12},{9,13},{1... | collective-permute-start | bytes 1572872 | tf_op jit(solution)/shard_map/ppermute | solution.py:14
  24.9 28.3 %collective-permute-start.1 = (bf16[2,128,2048]{2,1,0:T(8,128)(2,1)}, bf16[2,128,2048]{2,1,0:T(8,128)(2,1)}, u32[]{:S(2)}, u32[]{:S(2)}) collective-permute-start(bf16[2,128,2048]{2,1,0:T(8,128)(2,1)} %slice.173), channel_id=1, source_target_pairs={{0,2},{1,3},{2,4},{3,5},{4,6},{5,7},{6,8},{7,9},{8,10},{9,11},{10,... | collective-permute-start | bytes 3145736 | tf_op jit(solution)/shard_map/ppermute | solution.py:14
  26.5 6.9 %copy-start.2 = (bf16[1,256,2048]{2,1,0:T(8,128)(2,1)S(1)}, bf16[1,256,2048]{2,1,0:T(8,128)(2,1)}, u32[]{:S(2)}) copy-start(bf16[1,256,2048]{2,1,0:T(8,128)(2,1)} %param.17) | copy-start | bytes 3145732
  26.5 6.9 %copy-start.3 = (bf16[1,256,2048]{2,1,0:T(8,128)(2,1)S(1)}, bf16[1,256,2048]{2,1,0:T(8,128)(2,1)}, u32[]{:S(2)}) copy-start(bf16[1,256,2048]{2,1,0:T(8,128)(2,1)} %param.16) | copy-start | bytes 3145732
  44.0 15.1 %copy-start.5 = (bf16[16,256,128]{1,2,0:T(8,128)(2,1)S(1)}, bf16[16,256,128]{1,2,0:T(8,128)(2,1)}, u32[]{:S(2)}) copy-start(bf16[16,256,128]{1,2,0:T(8,128)(2,1)} %custom-call.5) | copy-start | bytes 3145732
  56.6 1.6 copy-start.4
  56.6 2.5 copy-start.8
  247.1 259.0 %all-reduce.2.cloned.1.call-start = ((), (), s32[]{:S(2)}) async-start(), calls=%async_computation.2 | async-start | bytes 1048576 | tf_op jit(solution)/shard_map/psum | solution.py:111
  272.0 13.7 %slice-start = ((s8[6029312]{0:T(1024)(128)(4,1)}), s8[1835008]{0:T(1024)(128)(4,1)S(1)}, s32[]{:S(2)}) async-start(s8[6029312]{0:T(1024)(128)(4,1)} %bitcast.107), calls=%async_computation.3 | async-start | bytes 3670016
  279.1 6.6 %slice-start.1 = ((s8[6029312]{0:T(1024)(128)(4,1)}), s8[4194304]{0:T(1024)(128)(4,1)S(1)}, s32[]{:S(2)}) async-start(s8[6029312]{0:T(1024)(128)(4,1)} %bitcast.107), calls=%async_computation.4 | async-start | bytes 8388608
  294.2 25.9 %copy-start.6 = (bf16[16,256,128]{2,1,0:T(8,128)(2,1)S(1)}, bf16[16,256,128]{2,1,0:T(8,128)(2,1)}, u32[]{:S(2)}) copy-start(bf16[16,256,128]{2,1,0:T(8,128)(2,1)} %get-tuple-element.112) | copy-start | bytes 3145732
  295.7 99.7 %collective-permute-start.4 = (bf16[2,256,2048]{2,1,0:T(8,128)(2,1)}, bf16[2,256,2048]{2,1,0:T(8,128)(2,1)}, u32[]{:S(2)}, u32[]{:S(2)}) collective-permute-start(bf16[2,256,2048]{2,1,0:T(8,128)(2,1)} %slice.202), channel_id=1, source_target_pairs={{1,0},{2,1},{3,2},{4,3},{5,4},{6,5},{7,6},{8,7},{9,8},{10,9},{11,1... | collective-permute-start | bytes 6291464 | tf_op jit(solution)/shard_map/ppermute | solution.py:14
  316.3 94.0 %collective-permute-start.5 = (bf16[2,128,2048]{2,1,0:T(8,128)(2,1)}, bf16[2,128,2048]{2,1,0:T(8,128)(2,1)S(1)}, u32[]{:S(2)}, u32[]{:S(2)}) collective-permute-start(bf16[2,128,2048]{2,1,0:T(8,128)(2,1)} %slice.204), channel_id=1, source_target_pairs={{2,0},{3,1},{4,2},{5,3},{6,4},{7,5},{8,6},{9,7},{10,8},{11,9},{12,... | collective-permute-start | bytes 3145736 | tf_op jit(solution)/shard_map/ppermute | solution.py:14
  320.1 2.0 copy-start.9
  320.1 10.7 %copy-start.7 = (bf16[2,64,2048]{2,1,0:T(8,128)(2,1)S(1)}, bf16[2,64,2048]{2,1,0:T(8,128)(2,1)}, u32[]{:S(2)}) copy-start(bf16[2,64,2048]{2,1,0:T(8,128)(2,1)} %slice.206) | copy-start | bytes 1572868
  322.0 93.0 %collective-permute-start.7 = (bf16[2,32,2048]{2,1,0:T(8,128)(2,1)S(1)}, bf16[2,32,2048]{2,1,0:T(8,128)(2,1)S(1)}, u32[]{:S(2)}, u32[]{:S(2)}) collective-permute-start(bf16[2,32,2048]{2,1,0:T(8,128)(2,1)S(1)} %copy-done.9), channel_id=1, source_target_pairs={{8,0},{9,1},{10,2},{11,3},{12,4},{13,5},{14,6},{15,7},{24,16},{25,... | collective-permute-start | bytes 786440 | tf_op jit(solution)/shard_map/ppermute | solution.py:14
  330.8 82.6 %collective-permute-start.6 = (bf16[2,64,2048]{2,1,0:T(8,128)(2,1)S(1)}, bf16[2,64,2048]{2,1,0:T(8,128)(2,1)S(1)}, u32[]{:S(2)}, u32[]{:S(2)}) collective-permute-start(bf16[2,64,2048]{2,1,0:T(8,128)(2,1)S(1)} %copy-done.7), channel_id=1, source_target_pairs={{4,0},{5,1},{6,2},{7,3},{8,4},{9,5},{10,6},{11,7},{12,8},{13,9},{1... | collective-permute-start | bytes 1572872 | tf_op jit(solution)/shard_map/ppermute | solution.py:14
  421.7 86.5 %copy-start.1 = (bf16[1,256,2048]{2,1,0:T(8,128)(2,1)S(1)}, bf16[1,256,2048]{2,1,0:T(8,128)(2,1)}, u32[]{:S(2)}) copy-start(bf16[1,256,2048]{2,1,0:T(8,128)(2,1)} %param.18) | copy-start | bytes 3145732
Sparse Core Ops, SparseCore 0:
  247.2 155.3 reduce-scatter.1
  418.0 88.0 all-reduce.1
where the time goes:
time: 520 us; the launch traced here: 515 us
  waiting for transfers between devices  170 us (33%)
  matrix products  165 us (32%)
  local copies, waits for them, and re-layouts  93.3 us (18%)
  starting transfers between devices  38.1 us (7%)
  other arithmetic  23.5 us (5%)
  between operations  14.4 us (3%)
  loops' own time  11 us (2%)
    ppermute x8, waiting for transfers between devices, shifted(): return lax.ppermute(block, axis, route)  88.9 us
    psum x1, waiting for transfers between devices, per_device(): weight_grad = lax.psum(partial_sum, 'dp').astype(jnp.float32)  81.2 us
    ppermute x8, starting transfers between devices, shifted(): return lax.ppermute(block, axis, route)  37.8 us
    dot_general x16, matrix products, attend_head(): jnp.dot(weights_low.T, grad_head, preferred_element_type=jnp.float32)  30.7 us
    dot_general x16, matrix products, attend_head(): jnp.dot(grad_scores, key_head, preferred_element_type=jnp.float32)  29.7 us
    dot_general x16, matrix products, attend_head(): jnp.dot(grad_scores.T, query_head, preferred_element_type=jnp.float32)  29.5 us
    dot_general x16, matrix products, attend_head(): jnp.dot(grad_head, value_head.T, preferred_element_type=jnp.float32)  21.1 us
    dot_general x16, matrix products, attend_head(): jnp.dot(weights_low, value_head, preferred_element_type=jnp.float32)  21 us
  transfers between devices with their start and end apart: 10, of which 5 were waited for; matrix products, arithmetic and copies ran while one was open for 19% of the time, Pallas kernels for 0%

commit v1 on v0

v1 whole, which is shorter than its diff:
```python
import functools
import math

import jax
import jax.numpy as jnp
from jax import lax
from jax.experimental import pallas as pl
from jax.experimental.pallas import tpu as pltpu
from jax.sharding import PartitionSpec as P

HEAD = 128
TOK = 256
GROUPS = 8
GW = 256
KEYS = 768
ROWS = (256, 128, 64, 32)
OFFS = (256, 512, 640, 704)
NSEQ = 16
NDP = 8
AHEAD = 3
MESH = pl.DeviceIdType.MESH
F32 = jnp.float32
BF16 = jnp.bfloat16


def dot(a, b, ca, cb):
    return lax.dot_general(a, b, (((ca,), (cb,)), ((), ())), preferred_element_type=F32)


def row_of(p):
    return jnp.where(
        p < 32,
        8 * p,
        jnp.where(
            p < 64, 8 * (p - 32) + 4, jnp.where(p < 128, 4 * (p - 64) + 2, 2 * (p - 128) + 1)
        ),
    )


def kernel(
    q_hbm, k_hbm, v_hbm, og_hbm, w_hbm,
    dq_hbm, dk_hbm, dv_hbm, wg_hbm,
    q_v, raw, og2, w_v, kvp, par, relay, ret, acc, att_own, att_out, att_in,
    zs, zr, ys, yr, xs, xr, wgp, dq_st, dkv_st, wg_st, bias, pm, pmt,
    ld, fs, fr, bs, br, ats, atr, ogs, zss, zrs, yss, yrs, xss, xrs, gss, grs, outs,
):
    scaling = 1.0 / math.sqrt(HEAD)
    factor = scaling * math.log2(math.e)
    dp, c = lax.axis_index("dp"), lax.axis_index("seq")
    z, xh = dp // 2, dp % 2
    y, xl, core = c // 4, (c // 2) % 2, c % 2
    even, odd = core == 0, core == 1
    sibling = c + 1 - 2 * core

    def remote(src, dst, ss, rs, to_dp, to_c):
        return pltpu.make_async_remote_copy(
            src_ref=src, dst_ref=dst, send_sem=ss, recv_sem=rs,
            device_id=(to_dp, to_c), device_id_type=MESH,
        )

    def load_kv(g, which):
        src = (k_hbm, v_hbm)[which]
        return pltpu.make_async_copy(
            src.at[0, :, pl.ds(g * GW, GW)], raw.at[g, :, pl.ds(which * GW, GW)], ld.at[g, which]
        )

    def load_q(g):
        return pltpu.make_async_copy(q_hbm.at[0, :, pl.ds(g * GW, GW)], q_v.at[g], ld.at[g, 2])

    def load_w(g):
        return pltpu.make_async_copy(w_hbm.at[pl.ds(g * GW, GW)], w_v.at[g], ld.at[g, 3])

    load_og = pltpu.make_async_copy(og_hbm.at[0], og2.at[0], ld.at[GROUPS, 0])

    partners = (
        [(dp, (c + d) % NSEQ) for d in (1, 15, 2, 14, 4, 8, 12)]
        + [((dp + d) % NDP, c) for d in range(1, NDP)]
        + [(dp + 1 - 2 * xh, c + 2 - 4 * xl)]
    )
    barrier = pltpu.get_barrier_semaphore()
    for partner in partners:
        pl.semaphore_signal(barrier, inc=1, device_id=partner, device_id_type=MESH)
    for g in range(GROUPS):
        load_kv(g, 0).start()
        load_kv(g, 1).start()
        if g == 0:
            load_og.start()
        load_q(g).start()
        load_w(g).start()

    pos0 = lax.broadcasted_iota(jnp.int32, (TOK, TOK), 0)
    pos1 = lax.broadcasted_iota(jnp.int32, (TOK, TOK), 1)
    pm[...] = (row_of(pos0) == pos1).astype(F32).astype(BF16)
    pmt[...] = (row_of(pos1) == pos0).astype(F32).astype(BF16)
    bias[0:TOK] = jnp.where(row_of(pos0) <= pos1, 0.0, -1e30).astype(F32)
    for level in range(4):
        shown = jnp.where(c >= 2**level, 0.0, -1e30).astype(F32)
        bias[pl.ds(OFFS[level], ROWS[level])] = jnp.full((ROWS[level], TOK), shown, F32)

        @pl.when(c < 2**level)
        def _():
            for g in range(GROUPS):
                kvp[g, pl.ds(OFFS[level], ROWS[level])] = jnp.zeros((ROWS[level], 2 * GW), BF16)

    bias[pl.ds(736, 32)] = jnp.full((32, TOK), -1e30, F32)
    for g in range(GROUPS):
        kvp[g, pl.ds(736, 32)] = jnp.zeros((32, 2 * GW), BF16)

    def fwd(g, level):
        return remote(
            kvp.at[g, pl.ds(0, ROWS[level])], kvp.at[g, pl.ds(OFFS[level], ROWS[level])],
            fs.at[g, level], fr.at[g, level], dp, (c + 2**level) % NSEQ,
        )

    def fwd_on(g):
        return remote(
            kvp.at[g, pl.ds(OFFS[0], ROWS[1])], kvp.at[g, pl.ds(OFFS[1], ROWS[1])],
            fs.at[g, 4], fr.at[g, 1], dp, sibling,
        )

    sends = (c < 15, jnp.logical_and(even, c < 14), c < 12, c < 8)
    takes = (c >= 1, c >= 2, c >= 4, c >= 8)
    hands_on = jnp.logical_and(even, c >= 2)

    def send_halos(g):
        load_kv(g, 0).wait()
        load_kv(g, 1).wait()
        kvp[g, pl.ds(0, TOK)] = dot(pm[...], raw[g], 1, 0).astype(BF16)
        for level in range(4):

            @pl.when(sends[level])
            def _():
                fwd(g, level).start()

    def bwd(g, level):
        return remote(
            par.at[g, pl.ds(OFFS[level] - TOK, ROWS[level])],
            ret.at[g, pl.ds(OFFS[level] - TOK, ROWS[level])],
            bs.at[g, level], br.at[g, level], dp, (c - 2**level + NSEQ) % NSEQ,
        )

    def bwd_relay(g):
        return remote(
            par.at[g, pl.ds(OFFS[1] - TOK, ROWS[1])], relay.at[g],
            bs.at[g, 1], br.at[g, 4], dp, sibling,
        )

    def send_back(g):
        @pl.when(odd)
        def _():
            bwd(g, 0).start()

        @pl.when(jnp.logical_and(odd, c >= 3))
        def _():
            bwd_relay(g).start()

        @pl.when(hands_on)
        def _():
            bwd(g, 1).start()

        @pl.when(c >= 4)
        def _():
            bwd(g, 2).start()

        @pl.when(c >= 8)
        def _():
            bwd(g, 3).start()

    def merge_back(g):
        @pl.when(hands_on)
        def _():
            bwd_relay(g).wait_recv()
            merged = par[g, pl.ds(0, ROWS[1])].astype(F32) + relay[g].astype(F32)
            par[g, pl.ds(0, ROWS[1])] = merged.astype(BF16)
            bwd(g, 0).start()

    comes_back = (c < 15, jnp.logical_and(even, c < 14), c < 12, c < 8)

    def store_kv(g, which):
        dst = (dk_hbm, dv_hbm)[which]
        return pltpu.make_async_copy(
            dkv_st.at[g, :, pl.ds(which * GW, GW)],
            dst.at[0, :, pl.ds(pl.multiple_of(g * GW, GW), GW)],
            outs.at[g, which],
        )

    def store_q(g):
        return pltpu.make_async_copy(
            dq_st.at[g], dq_hbm.at[0, :, pl.ds(pl.multiple_of(g * GW, GW), GW)], outs.at[g, 2]
        )

    def finish_kv(g):
        for level in range(4):

            @pl.when(comes_back[level])
            def _():
                bwd(g, level).wait_recv()
                acc[g, pl.ds(0, ROWS[level])] += ret[
                    g, pl.ds(OFFS[level] - TOK, ROWS[level])
                ].astype(F32)

        dkv_st[g] = dot(pmt[...], acc[g].astype(BF16), 1, 0).astype(BF16)
        store_kv(g, 0).start()
        store_kv(g, 1).start()

    def att_send(g):
        return remote(att_out.at[g], att_in.at[g], ats.at[g], atr.at[g], dp, sibling)

    og_send = remote(og2.at[0], og2.at[1], ogs.at[0], ogs.at[1], dp, sibling)

    def z_send(g, k):
        to = (z + k) % 4
        return remote(
            zs.at[g, to], zr.at[g, k - 1], zss.at[g, k - 1], zrs.at[g, k - 1], to * 2 + xh, c
        )

    def weight_terms(g):
        att_send(g).wait_recv()
        for part in range(4):
            cols = pl.ds(part * 512, 512)
            terms = dot(att_own[g], og2[0, :, cols], 1, 0) + dot(att_in[g], og2[1, :, cols], 1, 0)
            zs[g, part] = terms.astype(BF16)
        for k in (1, 2, 3):
            z_send(g, k).start()

    def y_send(g):
        k = (g // 2 - y + 4) % 4
        return remote(
            ys.at[g], yr.at[g % 2, k - 1], yss.at[g], yrs.at[g % 2, k - 1],
            dp, (g // 2) * 4 + c % 4,
        )

    def z_sum(g):
        total = zs[g, z].astype(F32)
        for k in (1, 2, 3):
            z_send(g, k).wait_recv()
        for k in (1, 2, 3):
            total = total + zr[g, k - 1].astype(F32)
        ys[g] = total.astype(BF16)

        @pl.when(g // 2 != y)
        def _():
            y_send(g).start()

    def x_send(j, half):
        k = (half * 2 + j - (xh * 2 + xl) + 4) % 4
        return k, remote(
            xs.at[j, half], xr.at[k - 1], xss.at[j * 2 + half], xrs.at[k - 1],
            z * 2 + half, y * 4 + j * 2 + core,
        )

    def y_sum():
        for j in (0, 1):
            total = ys[2 * y + j].astype(F32)
            for k in (1, 2, 3):
                remote(
                    yr.at[j, k - 1], yr.at[j, k - 1], yss.at[0], yrs.at[j, k - 1], dp, sibling
                ).wait_recv()
                total = total + yr[j, k - 1].astype(F32)
            for half in (0, 1):
                xs[j, half] = total[:, half * 256 : half * 256 + 256].astype(BF16)
                k, copy = x_send(j, half)

                @pl.when(k != 0)
                def _():
                    copy.start()

    def share(k):
        return remote(
            wgp.at[dp], wgp.at[dp], gss.at[k - 1], grs.at[k - 1], (dp + k) % NDP, c
        )

    def x_sum():
        total = xs[xl, xh].astype(F32)
        for k in (1, 2, 3):
            remote(xr.at[k - 1], xr.at[k - 1], xss.at[0], xrs.at[k - 1], dp, sibling).wait_recv()
            total = total + xr[k - 1].astype(F32)
        wgp[dp] = total.astype(BF16)
        for k in range(1, NDP):
            share(k).start()

    def group(g):
        load_q(g).wait()
        load_w(g).wait()
        grad_attn = dot(og2[0], w_v[g], 1, 1).astype(BF16)
        for hh in (0, 1):
            kcols = pl.ds(hh * HEAD, HEAD)
            vcols = pl.ds(GW + hh * HEAD, HEAD)
            keys, values = kvp[g, :, kcols], kvp[g, :, vcols]
            query = q_v[g, :, kcols]
            grad = grad_attn[:, hh * HEAD : (hh + 1) * HEAD]
            scores = dot(keys, query, 1, 1) + bias[...]
            top = jnp.max(scores, axis=0, keepdims=True)
            expo = jnp.exp2((scores - top) * factor)
            probs = expo * (1.0 / jnp.sum(expo, axis=0, keepdims=True))
            low = probs.astype(BF16)
            dprobs = dot(values, grad, 1, 1)
            inner = jnp.sum(probs * dprobs, axis=0, keepdims=True)
            dscores = (probs * (dprobs - inner)).astype(BF16)
            attended = dot(values, low, 0, 0).astype(BF16)

            @pl.when(core == hh)
            def _():
                att_own[g] = attended

            @pl.when(core != hh)
            def _():
                att_out[g] = attended

            grad_q = dot(keys, dscores, 0, 0) * scaling
            dq_st[g, :, kcols] = grad_q.T.astype(BF16)
            grad_k = dot(dscores, query, 1, 0) * scaling
            grad_v = dot(low, grad, 1, 0)
            acc[g, :, kcols] = grad_k[0:TOK]
            acc[g, :, vcols] = grad_v[0:TOK]
            par[g, :, kcols] = grad_k[TOK:736].astype(BF16)
            par[g, :, vcols] = grad_v[TOK:736].astype(BF16)

    pl.semaphore_wait(barrier, len(partners))
    for g in range(AHEAD):
        send_halos(g)
    load_og.wait()
    og_send.start()

    def step(g, carry):
        for level in range(4):

            @pl.when(takes[level])
            def _():
                fwd(g, level).wait_recv()

            if level == 0:

                @pl.when(hands_on)
                def _():
                    fwd_on(g).start()

        @pl.when(g + AHEAD < GROUPS)
        def _():
            send_halos(g + AHEAD)

        group(g)
        att_send(g).start()
        store_q(g).start()
        send_back(g)

        @pl.when(g >= 1)
        def _():
            merge_back(g - 1)

            @pl.when(g == 1)
            def _():
                og_send.wait_recv()

            weight_terms(g - 1)

        @pl.when(g >= 3)
        def _():
            z_sum(g - 3)

        return carry

    lax.fori_loop(0, GROUPS, step, 0)
    merge_back(GROUPS - 1)
    weight_terms(GROUPS - 1)

    def tail(g, carry):
        finish_kv(g)

        @pl.when(g < 3)
        def _():
            z_sum(g + GROUPS - 3)

        @pl.when(g == 4)
        def _():
            y_sum()

        @pl.when(g == 5)
        def _():
            x_sum()

        return carry

    lax.fori_loop(0, GROUPS, tail, 0)
    for k in range(1, NDP):
        come = wgp.at[(dp - k + NDP) % NDP]
        remote(come, come, gss.at[0], grs.at[k - 1], dp, sibling).wait_recv()
    for part in range(NDP):
        wg_st[:, pl.ds(part * 256, 256)] = wgp[part].astype(F32)
    wg_store = pltpu.make_async_copy(wg_st, wg_hbm, outs.at[GROUPS, 0])
    wg_store.start()

    og_send.wait_send()

    def drain(g, carry):
        store_q(g).wait()
        store_kv(g, 0).wait()
        store_kv(g, 1).wait()
        att_send(g).wait_send()
        for k in (1, 2, 3):
            z_send(g, k).wait_send()

        @pl.when(g // 2 != y)
        def _():
            y_send(g).wait_send()

        for level in range(4):

            @pl.when(sends[level])
            def _():
                fwd(g, level).wait_send()

        @pl.when(hands_on)
        def _():
            fwd_on(g).wait_send()
            bwd(g, 1).wait_send()

        @pl.when(c >= 1)
        def _():
            bwd(g, 0).wait_send()

        @pl.when(jnp.logical_and(odd, c >= 3))
        def _():
            bwd_relay(g).wait_send()

        @pl.when(c >= 4)
        def _():
            bwd(g, 2).wait_send()

        @pl.when(c >= 8)
        def _():
            bwd(g, 3).wait_send()

        return carry

    lax.fori_loop(0, GROUPS, drain, 0)
    for j in (0, 1):
        for half in (0, 1):
            k, copy = x_send(j, half)

            @pl.when(k != 0)
            def _():
                copy.wait_send()

    for k in range(1, NDP):
        share(k).wait_send()
    wg_store.wait()


def per_device(query_in, key_in, value_in, out_grad, out_weight):
    vm = pltpu.VMEM
    dma = pltpu.SemaphoreType.DMA
    g = GROUPS
    return pl.pallas_call(
        kernel,
        out_shape=(
            jax.ShapeDtypeStruct((1, TOK, 2048), BF16),
            jax.ShapeDtypeStruct((1, TOK, 2048), BF16),
            jax.ShapeDtypeStruct((1, TOK, 2048), BF16),
            jax.ShapeDtypeStruct((128, 2048), F32),
        ),
        in_specs=[pl.BlockSpec(memory_space=pl.ANY)] * 5,
        out_specs=(pl.BlockSpec(memory_space=pl.ANY),) * 4,
        scratch_shapes=[
            vm((g, TOK, GW), BF16),
            vm((g, TOK, 2 * GW), BF16),
            vm((2, TOK, 2048), BF16),
            vm((g, GW, 2048), BF16),
            vm((g, KEYS, 2 * GW), BF16),
            vm((g, 480, 2 * GW), BF16),
            vm((g, 128, 2 * GW), BF16),
            vm((g, 480, 2 * GW), BF16),
            vm((g, TOK, 2 * GW), F32),
            vm((g, HEAD, TOK), BF16),
            vm((g, HEAD, TOK), BF16),
            vm((g, HEAD, TOK), BF16),
            vm((g, 4, HEAD, 512), BF16),
            vm((g, 3, HEAD, 512), BF16),
            vm((g, HEAD, 512), BF16),
            vm((2, 3, HEAD, 512), BF16),
            vm((2, 2, HEAD, 256), BF16),
            vm((3, HEAD, 256), BF16),
            vm((NDP, HEAD, 256), BF16),
            vm((g, TOK, GW), BF16),
            vm((g, TOK, 2 * GW), BF16),
            vm((HEAD, 2048), F32),
            vm((KEYS, TOK), F32),
            vm((TOK, TOK), BF16),
            vm((TOK, TOK), BF16),
            dma((g + 1, 4)),
            dma((g, 5)),
            dma((g, 5)),
            dma((g, 5)),
            dma((g, 5)),
            dma((g,)),
            dma((g,)),
            dma((2,)),
            dma((g, 3)),
            dma((g, 3)),
            dma((g,)),
            dma((2, 3)),
            dma((4,)),
            dma((3,)),
            dma((NDP - 1,)),
            dma((NDP - 1,)),
            dma((g + 1, 3)),
        ],
        compiler_params=pltpu.CompilerParams(
            collective_id=0, has_side_effects=True, vmem_limit_bytes=60 * 2**20
        ),
        name="logsparse_backward",
    )(query_in, key_in, value_in, out_grad, out_weight)


def solution(mesh):
    return jax.shard_map(
        per_device,
        mesh=mesh,
        in_specs=(
            P("dp", "seq", None),
            P("dp", "seq", None),
            P("dp", "seq", None),
            P("dp", "seq", None),
            P(),
        ),
        out_specs=(
            P("dp", "seq", None),
            P("dp", "seq", None),
            P("dp", "seq", None),
            P("seq", None),
        ),
        check_vma=False,
    )
```

time: 520 us -> 119 us (0.23)
  the two profiles are of different devices: /device:TPU:26 before, /device:TPU:10 now
where the time goes in v1:
time: 119 us
  Pallas kernels  109 us (92%)
  local copies, waits for them, and re-layouts  9.21 us (8%)
    pallas_call x1, Pallas kernels, per_device(): pl.pallas_call(kernel, out_shape=(jax.ShapeDtypeStruct((1, TOK, 2048), BF...  109 us
    unnamed x4, local copies, waits for them, and re-layouts  9.21 us

profile of v1, /device:TPU:10, one launch (start us, length us, event | category | flops | bytes accessed | tf_op | source)
XLA Modules:
  0.0 119.0 jit_solution(16622850627420576575)
XLA Ops:
  0.6 109.1 %logsparse_backward.1 = (bf16[1,256,2048]{2,1,0:T(8,128)(2,1)}, bf16[1,256,2048]{2,1,0:T(8,128)(2,1)}, bf16[1,256,2048]{2,1,0:T(8,128)(2,1)}, f32[128,2048]{1,0:T(8,128)}) custom-call(bf16[1,256,2048]{2,1,0:T(8,128)(2,1)} %q_hbm.1, bf16[1,256,2048]{2,1,0:T(8,128)(2,1)} %k_hbm.1, bf16[1,256,2048]{2,1,0:T(8,128)(2,1)} %v_hbm.1, bf16[1,256,2048]{2,1,0:T(8,128)(2,1)} %og_hbm.1, ...), custom_call_target="tpu_custom_call" | custom-call | tf_op jit(solution)/shard_map/logsparse_backward/pallas_call | solution.py:454
  109.7 2.3 %copy.13 = bf16[1,256,2048]{2,1,0:T(8,128)(2,1)} copy(bf16[1,256,2048]{2,1,0:T(8,128)(2,1)} %get-tuple-element.8) | data formatting | bytes 2097152
  112.0 2.3 %copy.14 = bf16[1,256,2048]{2,1,0:T(8,128)(2,1)} copy(bf16[1,256,2048]{2,1,0:T(8,128)(2,1)} %get-tuple-element.9) | data formatting | bytes 2097152
  114.4 2.3 %copy.15 = bf16[1,256,2048]{2,1,0:T(8,128)(2,1)} copy(bf16[1,256,2048]{2,1,0:T(8,128)(2,1)} %get-tuple-element.10) | data formatting | bytes 2097152
  116.7 2.3 %copy.16 = f32[128,2048]{1,0:T(8,128)} copy(f32[128,2048]{1,0:T(8,128)} %get-tuple-element.11) | data formatting | bytes 2097152

commit v2 on v1

--- a/solution.py
+++ b/solution.py
@@ -18,6 +18,7 @@
 NSEQ = 16
 NDP = 8
 AHEAD = 3
+HOPS_B = 6
 MESH = pl.DeviceIdType.MESH
 F32 = jnp.float32
 BF16 = jnp.bfloat16
@@ -25,6 +26,10 @@
 
 def dot(a, b, ca, cb):
     return lax.dot_general(a, b, (((ca,), (cb,)), ((), ())), preferred_element_type=F32)
+
+
+def cols_of(g):
+    return pl.ds(pl.multiple_of(((g % 4) * 2 + g // 4) * GW, GW), GW)
 
 
 def row_of(p):
@@ -40,7 +45,7 @@
 def kernel(
     q_hbm, k_hbm, v_hbm, og_hbm, w_hbm,
     dq_hbm, dk_hbm, dv_hbm, wg_hbm,
-    q_v, raw, og2, w_v, kvp, par, relay, ret, acc, att_own, att_out, att_in,
+    q_v, raw, og2, w_v, kvp, par, relay, ret, acc, hop_f, hop_b, att_own, att_out, att_in,
     zs, zr, ys, yr, xs, xr, wgp, dq_st, dkv_st, wg_st, bias, pm, pmt,
     ld, fs, fr, bs, br, ats, atr, ogs, zss, zrs, yss, yrs, xss, xrs, gss, grs, outs,
 ):
@@ -61,19 +66,19 @@
     def load_kv(g, which):
         src = (k_hbm, v_hbm)[which]
         return pltpu.make_async_copy(
-            src.at[0, :, pl.ds(g * GW, GW)], raw.at[g, :, pl.ds(which * GW, GW)], ld.at[g, which]
+            src.at[0, :, cols_of(g)], raw.at[g, :, pl.ds(which * GW, GW)], ld.at[g, which]
         )
 
     def load_q(g):
-        return pltpu.make_async_copy(q_hbm.at[0, :, pl.ds(g * GW, GW)], q_v.at[g], ld.at[g, 2])
+        return pltpu.make_async_copy(q_hbm.at[0, :, cols_of(g)], q_v.at[g], ld.at[g, 2])
 
     def load_w(g):
-        return pltpu.make_async_copy(w_hbm.at[pl.ds(g * GW, GW)], w_v.at[g], ld.at[g, 3])
+        return pltpu.make_async_copy(w_hbm.at[cols_of(g)], w_v.at[g], ld.at[g, 3])
 
     load_og = pltpu.make_async_copy(og_hbm.at[0], og2.at[0], ld.at[GROUPS, 0])
 
     partners = (
-        [(dp, (c + d) % NSEQ) for d in (1, 15, 2, 14, 4, 8, 12)]
+        [(dp, (c + d) % NSEQ) for d in (1, 15, 2, 14, 3, 13, 4, 8, 12)]
         + [((dp + d) % NDP, c) for d in range(1, NDP)]
         + [(dp + 1 - 2 * xh, c + 2 - 4 * xl)]
     )
@@ -122,11 +127,45 @@
     takes = (c >= 1, c >= 2, c >= 4, c >= 8)
     hands_on = jnp.logical_and(even, c >= 2)
 
+    turns_f = jnp.logical_and(c % 4 == 3, c < 15)
+    hops_f = jnp.logical_and(c % 4 == 3, c >= 7)
+
+    def fwd_turn(g):
+        return remote(
+            kvp.at[g, pl.ds(0, TOK)], hop_f.at[g], fs.at[g, 0], fr.at[g, 4], dp, (c + 4) % NSEQ
+        )
+
+    def fwd_hop(g):
+        return remote(
+            hop_f.at[g], kvp.at[g, pl.ds(OFFS[0], TOK)], fs.at[g, 4], fr.at[g, 0],
+            dp, (c - 3 + NSEQ) % NSEQ,
+        )
+
+    def hop_on(g):
+        @pl.when(hops_f)
+        def _():
+            fwd_turn(g).wait_recv()
+            fwd_hop(g).start()
+
+    def send_level1(g):
+        @pl.when(sends[1])
+        def _():
+            fwd(g, 1).start()
+
     def send_halos(g):
         load_kv(g, 0).wait()
         load_kv(g, 1).wait()
         kvp[g, pl.ds(0, TOK)] = dot(pm[...], raw[g], 1, 0).astype(BF16)
-        for level in range(4):
+
+        @pl.when(turns_f)
+        def _():
+            fwd_turn(g).start()
+
+        @pl.when(jnp.logical_and(c % 4 != 3, sends[0]))
+        def _():
+            fwd(g, 0).start()
+
+        for level in (2, 3):
 
             @pl.when(sends[level])
             def _():
@@ -145,6 +184,20 @@
             bs.at[g, 1], br.at[g, 4], dp, sibling,
         )
 
+    def turns_b(g):
+        return jnp.logical_and(jnp.logical_and(c % 4 == 0, c >= 4), g < HOPS_B)
+
+    def bwd_turn(g):
+        return remote(
+            par.at[g, pl.ds(0, TOK)], hop_b.at[g], bs.at[g, 0], br.at[g, 5],
+            dp, (c - 4 + NSEQ) % NSEQ,
+        )
+
+    def bwd_hop(g):
+        return remote(
+            hop_b.at[g], ret.at[g, pl.ds(0, TOK)], bs.at[g, 5], br.at[g, 0], dp, (c + 3) % NSEQ
+        )
+
     def send_back(g):
         @pl.when(odd)
         def _():
@@ -172,7 +225,20 @@
             bwd_relay(g).wait_recv()
             merged = par[g, pl.ds(0, ROWS[1])].astype(F32) + relay[g].astype(F32)
             par[g, pl.ds(0, ROWS[1])] = merged.astype(BF16)
-            bwd(g, 0).start()
+
+            @pl.when(turns_b(g))
+            def _():
+                bwd_turn(g).start()
+
+            @pl.when(jnp.logical_not(turns_b(g)))
+            def _():
+                bwd(g, 0).start()
+
+    def hop_back(g):
+        @pl.when(jnp.logical_and(c % 4 == 0, c <= 8))
+        def _():
+            bwd_turn(g).wait_recv()
+            bwd_hop(g).start()
 
     comes_back = (c < 15, jnp.logical_and(even, c < 14), c < 12, c < 8)
 
@@ -180,13 +246,13 @@
         dst = (dk_hbm, dv_hbm)[which]
         return pltpu.make_async_copy(
             dkv_st.at[g, :, pl.ds(which * GW, GW)],
-            dst.at[0, :, pl.ds(pl.multiple_of(g * GW, GW), GW)],
+            dst.at[0, :, cols_of(g)],
             outs.at[g, which],
         )
 
     def store_q(g):
         return pltpu.make_async_copy(
-            dq_st.at[g], dq_hbm.at[0, :, pl.ds(pl.multiple_of(g * GW, GW), GW)], outs.at[g, 2]
+            dq_st.at[g], dq_hbm.at[0, :, cols_of(g)], outs.at[g, 2]
         )
 
     def finish_kv(g):
@@ -224,10 +290,10 @@
             z_send(g, k).start()
 
     def y_send(g):
-        k = (g // 2 - y + 4) % 4
-        return remote(
-            ys.at[g], yr.at[g % 2, k - 1], yss.at[g], yrs.at[g % 2, k - 1],
-            dp, (g // 2) * 4 + c % 4,
+        k = (g % 4 - y + 4) % 4
+        return remote(
+            ys.at[g], yr.at[g // 4, k - 1], yss.at[g], yrs.at[g // 4, k - 1],
+            dp, (g % 4) * 4 + c % 4,
         )
 
     def z_sum(g):
@@ -238,7 +304,7 @@
             total = total + zr[g, k - 1].astype(F32)
         ys[g] = total.astype(BF16)
 
-        @pl.when(g // 2 != y)
+        @pl.when(g % 4 != y)
         def _():
             y_send(g).start()
 
@@ -251,7 +317,7 @@
 
     def y_sum():
         for j in (0, 1):
-            total = ys[2 * y + j].astype(F32)
+            total = ys[y + 4 * j].astype(F32)
             for k in (1, 2, 3):
                 remote(
                     yr.at[j, k - 1], yr.at[j, k - 1], yss.at[0], yrs.at[j, k - 1], dp, sibling
@@ -317,10 +383,14 @@
             par[g, :, vcols] = grad_v[TOK:736].astype(BF16)
 
     pl.semaphore_wait(barrier, len(partners))
-    for g in range(AHEAD):
+    for g in range(GROUPS):
         send_halos(g)
-    load_og.wait()
-    og_send.start()
+        if g < AHEAD:
+            send_level1(g)
+        if g == 0:
+            load_og.wait()
+            og_send.start()
+    hop_on(0)
 
     def step(g, carry):
         for level in range(4):
@@ -337,13 +407,17 @@
 
         @pl.when(g + AHEAD < GROUPS)
         def _():
-            send_halos(g + AHEAD)
+            send_level1(g + AHEAD)
 
         group(g)
         att_send(g).start()
         store_q(g).start()
         send_back(g)
 
+        @pl.when(g + 1 < GROUPS)
+        def _():
+            hop_on(g + 1)
+
         @pl.when(g >= 1)
         def _():
             merge_back(g - 1)
@@ -356,6 +430,7 @@
 
         @pl.when(g >= 3)
         def _():
+            hop_back(g - 3)
             z_sum(g - 3)
 
         return carry
@@ -364,21 +439,22 @@
     merge_back(GROUPS - 1)
     weight_terms(GROUPS - 1)
 
+    hop_back(HOPS_B - 1)
+
     def tail(g, carry):
+        @pl.when(g < 3)
+        def _():
+            z_sum(g + GROUPS - 3)
+
+        @pl.when(g == 4)
+        def _():
+            y_sum()
+
+        @pl.when(g == 5)
+        def _():
+            x_sum()
+
         finish_kv(g)
-
-        @pl.when(g < 3)
-        def _():
-            z_sum(g + GROUPS - 3)
-
-        @pl.when(g == 4)
-        def _():
-            y_sum()
-
-        @pl.when(g == 5)
-        def _():
-            x_sum()
-
         return carry
 
     lax.fori_loop(0, GROUPS, tail, 0)
@@ -400,7 +476,7 @@
         for k in (1, 2, 3):
             z_send(g, k).wait_send()
 
-        @pl.when(g // 2 != y)
+        @pl.when(g % 4 != y)
         def _():
             y_send(g).wait_send()
 
@@ -409,6 +485,14 @@
             @pl.when(sends[level])
             def _():
                 fwd(g, level).wait_send()
+
+        @pl.when(hops_f)
+        def _():
+            fwd_hop(g).wait_send()
+
+        @pl.when(jnp.logical_and(jnp.logical_and(c % 4 == 0, c <= 8), g < HOPS_B))
+        def _():
+            bwd_hop(g).wait_send()
 
         @pl.when(hands_on)
         def _():
@@ -447,11 +531,42 @@
     wg_store.wait()
 
 
+def move_kernel(*refs):
+    ins, outs, bufs, sems = refs[:4], refs[4:8], refs[8:12], refs[12]
+    first, second = [], []
+    for i in range(4):
+        a, b = (ins[i].at[0], outs[i].at[0]) if i < 3 else (ins[i], outs[i])
+        n = a.shape[0] // 2
+        for j in range(2):
+            rows = pl.ds(j * n, n)
+            first.append(pltpu.make_async_copy(a.at[rows], bufs[i].at[rows], sems.at[0, i, j]))
+            second.append(pltpu.make_async_copy(bufs[i].at[rows], b.at[rows], sems.at[1, i, j]))
+    for copy in first:
+        copy.start()
+    for copy, then in zip(first, second):
+        copy.wait()
+        then.start()
+    for copy in second:
+        copy.wait()
+
+
+def move_out(results):
+    return pl.pallas_call(
+        move_kernel,
+        out_shape=tuple(jax.ShapeDtypeStruct(r.shape, r.dtype) for r in results),
+        in_specs=[pl.BlockSpec(memory_space=pl.ANY)] * 4,
+        out_specs=(pl.BlockSpec(memory_space=pl.ANY),) * 4,
+        scratch_shapes=[pltpu.VMEM(r.shape[-2:], r.dtype) for r in results]
+        + [pltpu.SemaphoreType.DMA((2, 4, 2))],
+        name="move_out",
+    )(*results)
+
+
 def per_device(query_in, key_in, value_in, out_grad, out_weight):
     vm = pltpu.VMEM
     dma = pltpu.SemaphoreType.DMA
     g = GROUPS
-    return pl.pallas_call(
+    results = pl.pallas_call(
         kernel,
         out_shape=(
             jax.ShapeDtypeStruct((1, TOK, 2048), BF16),
@@ -471,6 +586,8 @@
             vm((g, 128, 2 * GW), BF16),
             vm((g, 480, 2 * GW), BF16),
             vm((g, TOK, 2 * GW), F32),
+            vm((g, TOK, 2 * GW), BF16),
+            vm((HOPS_B, TOK, 2 * GW), BF16),
             vm((g, HEAD, TOK), BF16),
             vm((g, HEAD, TOK), BF16),
             vm((g, HEAD, TOK), BF16),
@@ -490,8 +607,8 @@
             dma((g + 1, 4)),
             dma((g, 5)),
             dma((g, 5)),
-            dma((g, 5)),
-            dma((g, 5)),
+            dma((g, 6)),
+            dma((g, 6)),
             dma((g,)),
             dma((g,)),
             dma((2,)),
@@ -510,6 +627,7 @@
         ),
         name="logsparse_backward",
     )(query_in, key_in, value_in, out_grad, out_weight)
+    return move_out(results)
 
 
 def solution(mesh):

time: 119 us -> 104 us (0.87)
  the two profiles are of different devices: /device:TPU:10 before, /device:TPU:26 now
where the time goes in v2:
time: 104 us
  Pallas kernels  103 us (99%)
    pallas_call x1, Pallas kernels, per_device(): pl.pallas_call(kernel, out_shape=(jax.ShapeDtypeStruct((1, TOK, 2048), BF...  99.4 us
    pallas_call x1, Pallas kernels, move_out(): pl.pallas_call(move_kernel, out_shape=tuple((jax.ShapeDtypeStruct(r.shape...  3.58 us

profile of v2, /device:TPU:26, one launch (start us, length us, event | category | flops | bytes accessed | tf_op | source)
XLA Modules:
  0.0 103.6 jit_solution(3270529461524315446)
XLA Ops:
  0.6 99.4 %logsparse_backward.1 = (bf16[1,256,2048]{2,1,0:T(8,128)(2,1)}, bf16[1,256,2048]{2,1,0:T(8,128)(2,1)}, bf16[1,256,2048]{2,1,0:T(8,128)(2,1)}, f32[128,2048]{1,0:T(8,128)}) custom-call(bf16[1,256,2048]{2,1,0:T(8,128)(2,1)} %q_hbm.1, bf16[1,256,2048]{2,1,0:T(8,128)(2,1)} %k_hbm.1, bf16[1,256,2048]{2,1,0:T(8,128)(2,1)} %v_hbm.1, bf16[1,256,2048]{2,1,0:T(8,128)(2,1)} %og_hbm.1, ...), custom_call_target="tpu_custom_call" | custom-call | tf_op jit(solution)/shard_map/logsparse_backward/pallas_call | solution.py:569
  100.1 3.6 %move_out.1 = (bf16[1,256,2048]{2,1,0:T(8,128)(2,1)}, bf16[1,256,2048]{2,1,0:T(8,128)(2,1)}, bf16[1,256,2048]{2,1,0:T(8,128)(2,1)}, f32[128,2048]{1,0:T(8,128)}) custom-call(bf16[1,256,2048]{2,1,0:T(8,128)(2,1)} %get-tuple-element.8.refs_0_, bf16[1,256,2048]{2,1,0:T(8,128)(2,1)} %get-tuple-element.9.refs_1_, ...), custom_call_target="tpu_custom_call" | custom-call | tf_op jit(solution)/shard_map/move_out/pallas_call | solution.py:554

commit v3 on v2

--- a/solution.py
+++ b/solution.py
@@ -18,6 +18,8 @@
 NSEQ = 16
 NDP = 8
 AHEAD = 3
+LATE = 1
+LAG2, LAG3 = 3, 5
 HOPS_B = 6
 MESH = pl.DeviceIdType.MESH
 F32 = jnp.float32
@@ -46,8 +48,8 @@
     q_hbm, k_hbm, v_hbm, og_hbm, w_hbm,
     dq_hbm, dk_hbm, dv_hbm, wg_hbm,
     q_v, raw, og2, w_v, kvp, par, relay, ret, acc, hop_f, hop_b, att_own, att_out, att_in,
-    zs, zr, ys, yr, xs, xr, wgp, dq_st, dkv_st, wg_st, bias, pm, pmt,
-    ld, fs, fr, bs, br, ats, atr, ogs, zss, zrs, yss, yrs, xss, xrs, gss, grs, outs,
+    wa, wb, zr_a, xa, xs_a, xr_a, xr_b, zs_b, zr_b, ys, yr, xm, xs, xr, wgp, dq_st, dkv_st, wg_st, bias, pm, pmt,
+    ld, fs, fr, bs, br, ats, atr, ogs, zas, zar, zbs, zbr, xas, xar, yss, yrs, xss, gss, grs, outs,
 ):
     scaling = 1.0 / math.sqrt(HEAD)
     factor = scaling * math.log2(math.e)
@@ -198,6 +200,8 @@
             hop_b.at[g], ret.at[g, pl.ds(0, TOK)], bs.at[g, 5], br.at[g, 0], dp, (c + 3) % NSEQ
         )
 
+    late = c % 4 == 2
+
     def send_back(g):
         @pl.when(odd)
         def _():
@@ -207,7 +211,7 @@
         def _():
             bwd_relay(g).start()
 
-        @pl.when(hands_on)
+        @pl.when(jnp.logical_and(hands_on, jnp.logical_not(late)))
         def _():
             bwd(g, 1).start()
 
@@ -233,6 +237,10 @@
             @pl.when(jnp.logical_not(turns_b(g)))
             def _():
                 bwd(g, 0).start()
+
+    def late_back(g):
+        bwd(g, 1).start()
+        merge_back(g)
 
     def hop_back(g):
         @pl.when(jnp.logical_and(c % 4 == 0, c <= 8))
@@ -274,20 +282,57 @@
 
     og_send = remote(og2.at[0], og2.at[1], ogs.at[0], ogs.at[1], dp, sibling)
 
-    def z_send(g, k):
+    def z_send_a(g, k):
         to = (z + k) % 4
         return remote(
-            zs.at[g, to], zr.at[g, k - 1], zss.at[g, k - 1], zrs.at[g, k - 1], to * 2 + xh, c
-        )
+            wa.at[g, to], zr_a.at[g, k - 1], zas.at[g, k - 1], zar.at[g, k - 1], to * 2 + xh, c
+        )
+
+    def z_send_b(g, k):
+        to = (z + k) % 4
+        return remote(
+            zs_b.at[g, to], zr_b.at[g, k - 1], zbs.at[g, k - 1], zbr.at[g, k - 1], to * 2 + xh, c
+        )
+
+    across = (dp + 1 - 2 * xh, c + 2 - 4 * xl)
+
+    def x_send_a(g):
+        return remote(xs_a.at[g], xr_a.at[g], xas.at[g, 0], xar.at[g, 0], *across)
+
+    def x_send_b(g):
+        return remote(wb.at[g, 1 - xh], xr_b.at[g], xas.at[g, 1], xar.at[g, 1], *across)
 
     def weight_terms(g):
         att_send(g).wait_recv()
         for part in range(4):
             cols = pl.ds(part * 512, 512)
             terms = dot(att_own[g], og2[0, :, cols], 1, 0) + dot(att_in[g], og2[1, :, cols], 1, 0)
-            zs[g, part] = terms.astype(BF16)
+            terms = terms.astype(BF16)
+            if part < 2:
+                wa[g, 2 * part] = terms[:, 0:256]
+                wa[g, 2 * part + 1] = terms[:, 256:512]
+            else:
+                for q in range(4):
+                    wb[g, q % 2, 2 * (part - 2) + q // 2] = terms[:, q * 128 : q * 128 + 128]
         for k in (1, 2, 3):
-            z_send(g, k).start()
+            z_send_a(g, k).start()
+        x_send_b(g).start()
+
+    def second_sums(g):
+        for k in (1, 2, 3):
+            z_send_a(g, k).wait_recv()
+        total = wa[g, z].astype(F32)
+        for k in (1, 2, 3):
+            total = total + zr_a[g, k - 1].astype(F32)
+        left, right = total[:, 0:128], total[:, 128:256]
+        xa[g] = jnp.where(xh == 0, left, right)
+        xs_a[g] = jnp.where(xh == 0, right, left).astype(BF16)
+        x_send_a(g).start()
+        x_send_b(g).wait_recv()
+        for part in range(4):
+            zs_b[g, part] = (wb[g, xh, part].astype(F32) + xr_b[g, part].astype(F32)).astype(BF16)
+        for k in (1, 2, 3):
+            z_send_b(g, k).start()
 
     def y_send(g):
         k = (g % 4 - y + 4) % 4
@@ -296,26 +341,24 @@
             dp, (g % 4) * 4 + c % 4,
         )
 
-    def z_sum(g):
-        total = zs[g, z].astype(F32)
+    def third_sums(g):
+        x_send_a(g).wait_recv()
         for k in (1, 2, 3):
-            z_send(g, k).wait_recv()
+            z_send_b(g, k).wait_recv()
+        ys[g, :, 0:128] = (xa[g] + xr_a[g].astype(F32)).astype(BF16)
+        total = zs_b[g, z].astype(F32)
         for k in (1, 2, 3):
-            total = total + zr[g, k - 1].astype(F32)
-        ys[g] = total.astype(BF16)
+            total = total + zr_b[g, k - 1].astype(F32)
+        ys[g, :, 128:256] = total.astype(BF16)
 
         @pl.when(g % 4 != y)
         def _():
             y_send(g).start()
 
-    def x_send(j, half):
-        k = (half * 2 + j - (xh * 2 + xl) + 4) % 4
-        return k, remote(
-            xs.at[j, half], xr.at[k - 1], xss.at[j * 2 + half], xrs.at[k - 1],
-            z * 2 + half, y * 4 + j * 2 + core,
-        )
+    x_send = remote(xs, xr, xss.at[0], xss.at[1], dp, c + 2 - 4 * xl)
 
     def y_sum():
+        totals = []
         for j in (0, 1):
             total = ys[y + 4 * j].astype(F32)
             for k in (1, 2, 3):
@@ -323,13 +366,10 @@
                     yr.at[j, k - 1], yr.at[j, k - 1], yss.at[0], yrs.at[j, k - 1], dp, sibling
                 ).wait_recv()
                 total = total + yr[j, k - 1].astype(F32)
-            for half in (0, 1):
-                xs[j, half] = total[:, half * 256 : half * 256 + 256].astype(BF16)
-                k, copy = x_send(j, half)
-
-                @pl.when(k != 0)
-                def _():
-                    copy.start()
+            totals.append(total)
+        xm[...] = jnp.where(xl == 0, totals[0], totals[1])
+        xs[...] = jnp.where(xl == 0, totals[1], totals[0]).astype(BF16)
+        x_send.start()
 
     def share(k):
         return remote(
@@ -337,11 +377,8 @@
         )
 
     def x_sum():
-        total = xs[xl, xh].astype(F32)
-        for k in (1, 2, 3):
-            remote(xr.at[k - 1], xr.at[k - 1], xss.at[0], xrs.at[k - 1], dp, sibling).wait_recv()
-            total = total + xr[k - 1].astype(F32)
-        wgp[dp] = total.astype(BF16)
+        x_send.wait_recv()
+        wgp[dp] = (xm[...] + xr[...].astype(F32)).astype(BF16)
         for k in range(1, NDP):
             share(k).start()
 
@@ -418,51 +455,83 @@
         def _():
             hop_on(g + 1)
 
+        @pl.when(jnp.logical_and(g >= 1, jnp.logical_not(late)))
+        def _():
+            merge_back(g - 1)
+
+        @pl.when(jnp.logical_and(g >= LATE, late))
+        def _():
+            late_back(g - LATE)
+
+        @pl.when(g == 1)
+        def _():
+            og_send.wait_recv()
+
         @pl.when(g >= 1)
         def _():
-            merge_back(g - 1)
-
-            @pl.when(g == 1)
-            def _():
-                og_send.wait_recv()
-
             weight_terms(g - 1)
 
         @pl.when(g >= 3)
         def _():
             hop_back(g - 3)
-            z_sum(g - 3)
+
+        @pl.when(g >= LAG2)
+        def _():
+            second_sums(g - LAG2)
+
+        @pl.when(g >= LAG3)
+        def _():
+            third_sums(g - LAG3)
 
         return carry
 
     lax.fori_loop(0, GROUPS, step, 0)
-    merge_back(GROUPS - 1)
+
+    @pl.when(jnp.logical_not(late))
+    def _():
+        merge_back(GROUPS - 1)
+
     weight_terms(GROUPS - 1)
 
+    @pl.when(late)
+    def _():
+        lax.fori_loop(GROUPS - LATE, GROUPS, lambda g, carry: late_back(g) or carry, 0)
+
     hop_back(HOPS_B - 1)
 
-    def tail(g, carry):
-        @pl.when(g < 3)
-        def _():
-            z_sum(g + GROUPS - 3)
-
-        @pl.when(g == 4)
+    def tail(i, carry):
+        @pl.when(jnp.logical_and(i >= GROUPS, i < GROUPS + LAG2))
+        def _():
+            second_sums(i - LAG2)
+
+        @pl.when(i < GROUPS + LAG3)
+        def _():
+            third_sums(i - LAG3)
+
+        return carry
+
+    lax.fori_loop(GROUPS, GROUPS + LAG3, tail, 0)
+
+    def last(g, carry):
+        finish_kv(g)
+
+        @pl.when(g == 1)
         def _():
             y_sum()
 
-        @pl.when(g == 5)
+        @pl.when(g == 3)
         def _():
             x_sum()
 
-        finish_kv(g)
         return carry
 
-    lax.fori_loop(0, GROUPS, tail, 0)
+    lax.fori_loop(0, GROUPS, last, 0)
     for k in range(1, NDP):
         come = wgp.at[(dp - k + NDP) % NDP]
         remote(come, come, gss.at[0], grs.at[k - 1], dp, sibling).wait_recv()
     for part in range(NDP):
-        wg_st[:, pl.ds(part * 256, 256)] = wgp[part].astype(F32)
+        wg_st[:, pl.ds(part * 128, 128)] = wgp[part, :, 0:128].astype(F32)
+        wg_st[:, pl.ds(1024 + part * 128, 128)] = wgp[part, :, 128:256].astype(F32)
     wg_store = pltpu.make_async_copy(wg_st, wg_hbm, outs.at[GROUPS, 0])
     wg_store.start()
 
@@ -474,7 +543,10 @@
         store_kv(g, 1).wait()
         att_send(g).wait_send()
         for k in (1, 2, 3):
-            z_send(g, k).wait_send()
+            z_send_a(g, k).wait_send()
+            z_send_b(g, k).wait_send()
+        x_send_a(g).wait_send()
+        x_send_b(g).wait_send()
 
         @pl.when(g % 4 != y)
         def _():
@@ -518,14 +590,7 @@
         return carry
 
     lax.fori_loop(0, GROUPS, drain, 0)
-    for j in (0, 1):
-        for half in (0, 1):
-            k, copy = x_send(j, half)
-
-            @pl.when(k != 0)
-            def _():
-                copy.wait_send()
-
+    x_send.wait_send()
     for k in range(1, NDP):
         share(k).wait_send()
     wg_store.wait()
@@ -591,12 +656,20 @@
             vm((g, HEAD, TOK), BF16),
             vm((g, HEAD, TOK), BF16),
             vm((g, HEAD, TOK), BF16),
-            vm((g, 4, HEAD, 512), BF16),
-            vm((g, 3, HEAD, 512), BF16),
-            vm((g, HEAD, 512), BF16),
-            vm((2, 3, HEAD, 512), BF16),
-            vm((2, 2, HEAD, 256), BF16),
-            vm((3, HEAD, 256), BF16),
+            vm((g, 4, HEAD, 256), BF16),
+            vm((g, 2, 4, HEAD, 128), BF16),
+            vm((g, 3, HEAD, 256), BF16),
+            vm((g, HEAD, 128), F32),
+            vm((g, HEAD, 128), BF16),
+            vm((g, HEAD, 128), BF16),
+            vm((g, 4, HEAD, 128), BF16),
+            vm((g, 4, HEAD, 128), BF16),
+            vm((g, 3, HEAD, 128), BF16),
+            vm((g, HEAD, 256), BF16),
+            vm((2, 3, HEAD, 256), BF16),
+            vm((HEAD, 256), F32),
+            vm((HEAD, 256), BF16),
+            vm((HEAD, 256), BF16),
             vm((NDP, HEAD, 256), BF16),
             vm((g, TOK, GW), BF16),
             vm((g, TOK, 2 * GW), BF16),
@@ -614,10 +687,13 @@
             dma((2,)),
             dma((g, 3)),
             dma((g, 3)),
+            dma((g, 3)),
+            dma((g, 3)),
+            dma((g, 2)),
+            dma((g, 2)),
             dma((g,)),
             dma((2, 3)),
-            dma((4,)),
-            dma((3,)),
+            dma((2,)),
             dma((NDP - 1,)),
             dma((NDP - 1,)),
             dma((g + 1, 3)),

time: 104 us -> 103 us (level)
  no operation moved by 1% of the time
where the time goes in v3:
time: 103 us
  Pallas kernels  102 us (99%)
    pallas_call x1, Pallas kernels, per_device(): pl.pallas_call(kernel, out_shape=(jax.ShapeDtypeStruct((1, TOK, 2048), BF...  98.7 us
    pallas_call x1, Pallas kernels, move_out(): pl.pallas_call(move_kernel, out_shape=tuple((jax.ShapeDtypeStruct(r.shape...  3.58 us

profile of v3, /device:TPU:26, one launch (start us, length us, event | category | flops | bytes accessed | tf_op | source)
XLA Modules:
  0.0 103.0 jit_solution(16536629150625011851)
XLA Ops:
  0.6 98.7 %logsparse_backward.1 = (bf16[1,256,2048]{2,1,0:T(8,128)(2,1)}, bf16[1,256,2048]{2,1,0:T(8,128)(2,1)}, bf16[1,256,2048]{2,1,0:T(8,128)(2,1)}, f32[128,2048]{1,0:T(8,128)}) custom-call(bf16[1,256,2048]{2,1,0:T(8,128)(2,1)} %q_hbm.1, bf16[1,256,2048]{2,1,0:T(8,128)(2,1)} %k_hbm.1, bf16[1,256,2048]{2,1,0:T(8,128)(2,1)} %v_hbm.1, bf16[1,256,2048]{2,1,0:T(8,128)(2,1)} %og_hbm.1, ...), custom_call_target="tpu_custom_call" | custom-call | tf_op jit(solution)/shard_map/logsparse_backward/pallas_call | solution.py:634
  99.4 3.6 %move_out.1 = (bf16[1,256,2048]{2,1,0:T(8,128)(2,1)}, bf16[1,256,2048]{2,1,0:T(8,128)(2,1)}, bf16[1,256,2048]{2,1,0:T(8,128)(2,1)}, f32[128,2048]{1,0:T(8,128)}) custom-call(bf16[1,256,2048]{2,1,0:T(8,128)(2,1)} %get-tuple-element.8.refs_0_, bf16[1,256,2048]{2,1,0:T(8,128)(2,1)} %get-tuple-element.9.refs_1_, ...), custom_call_target="tpu_custom_call" | custom-call | tf_op jit(solution)/shard_map/move_out/pallas_call | solution.py:619

commit v4 on v3

--- a/solution.py
+++ b/solution.py
@@ -530,8 +530,8 @@
         come = wgp.at[(dp - k + NDP) % NDP]
         remote(come, come, gss.at[0], grs.at[k - 1], dp, sibling).wait_recv()
     for part in range(NDP):
-        wg_st[:, pl.ds(part * 128, 128)] = wgp[part, :, 0:128].astype(F32)
-        wg_st[:, pl.ds(1024 + part * 128, 128)] = wgp[part, :, 128:256].astype(F32)
+        wg_st[:, pl.ds(part * 128, 128)] = wgp[part, :, 0:128]
+        wg_st[:, pl.ds(1024 + part * 128, 128)] = wgp[part, :, 128:256]
     wg_store = pltpu.make_async_copy(wg_st, wg_hbm, outs.at[GROUPS, 0])
     wg_store.start()
 
@@ -597,19 +597,23 @@
 
 
 def move_kernel(*refs):
-    ins, outs, bufs, sems = refs[:4], refs[4:8], refs[8:12], refs[12]
+    ins, outs, bufs, wide, sems = refs[:4], refs[4:8], refs[8:12], refs[12], refs[13]
     first, second = [], []
-    for i in range(4):
+    for i in (3, 0, 1, 2):
         a, b = (ins[i].at[0], outs[i].at[0]) if i < 3 else (ins[i], outs[i])
         n = a.shape[0] // 2
         for j in range(2):
             rows = pl.ds(j * n, n)
             first.append(pltpu.make_async_copy(a.at[rows], bufs[i].at[rows], sems.at[0, i, j]))
-            second.append(pltpu.make_async_copy(bufs[i].at[rows], b.at[rows], sems.at[1, i, j]))
+            src = wide if i == 3 else bufs[i]
+            second.append(pltpu.make_async_copy(src.at[rows], b.at[rows], sems.at[1, i, j]))
     for copy in first:
         copy.start()
-    for copy, then in zip(first, second):
+    for at, (copy, then) in enumerate(zip(first, second)):
         copy.wait()
+        if at < 2:
+            rows = pl.ds(at * 64, 64)
+            wide[rows] = bufs[3][rows].astype(F32)
         then.start()
     for copy in second:
         copy.wait()
@@ -618,11 +622,12 @@
 def move_out(results):
     return pl.pallas_call(
         move_kernel,
-        out_shape=tuple(jax.ShapeDtypeStruct(r.shape, r.dtype) for r in results),
+        out_shape=tuple(jax.ShapeDtypeStruct(r.shape, r.dtype) for r in results[:3])
+        + (jax.ShapeDtypeStruct(results[3].shape, F32),),
         in_specs=[pl.BlockSpec(memory_space=pl.ANY)] * 4,
         out_specs=(pl.BlockSpec(memory_space=pl.ANY),) * 4,
         scratch_shapes=[pltpu.VMEM(r.shape[-2:], r.dtype) for r in results]
-        + [pltpu.SemaphoreType.DMA((2, 4, 2))],
+        + [pltpu.VMEM(results[3].shape, F32), pltpu.SemaphoreType.DMA((2, 4, 2))],
         name="move_out",
     )(*results)
 
@@ -637,7 +642,7 @@
             jax.ShapeDtypeStruct((1, TOK, 2048), BF16),
             jax.ShapeDtypeStruct((1, TOK, 2048), BF16),
             jax.ShapeDtypeStruct((1, TOK, 2048), BF16),
-            jax.ShapeDtypeStruct((128, 2048), F32),
+            jax.ShapeDtypeStruct((128, 2048), BF16),
         ),
         in_specs=[pl.BlockSpec(memory_space=pl.ANY)] * 5,
         out_specs=(pl.BlockSpec(memory_space=pl.ANY),) * 4,
@@ -673,7 +678,7 @@
             vm((NDP, HEAD, 256), BF16),
             vm((g, TOK, GW), BF16),
             vm((g, TOK, 2 * GW), BF16),
-            vm((HEAD, 2048), F32),
+            vm((HEAD, 2048), BF16),
             vm((KEYS, TOK), F32),
             vm((TOK, TOK), BF16),
             vm((TOK, TOK), BF16),

time: 103 us -> 103 us (level)
  no operation moved by 1% of the time
where the time goes in v4:
time: 103 us; the launch traced here: 102 us
  Pallas kernels  102 us (99%)
    pallas_call x1, Pallas kernels, per_device(): pl.pallas_call(kernel, out_shape=(jax.ShapeDtypeStruct((1, TOK, 2048), BF...  98.6 us
    pallas_call x1, Pallas kernels, move_out(): pl.pallas_call(move_kernel, out_shape=tuple((jax.ShapeDtypeStruct(r.shape...  3.19 us

profile of v4, /device:TPU:26, one launch (start us, length us, event | category | flops | bytes accessed | tf_op | source)
XLA Modules:
  0.0 102.4 jit_solution(13999190680178448009)
XLA Ops:
  0.6 98.6 %logsparse_backward.1 = (bf16[1,256,2048]{2,1,0:T(8,128)(2,1)}, bf16[1,256,2048]{2,1,0:T(8,128)(2,1)}, bf16[1,256,2048]{2,1,0:T(8,128)(2,1)}, bf16[128,2048]{1,0:T(8,128)(2,1)}) custom-call(bf16[1,256,2048]{2,1,0:T(8,128)(2,1)} %q_hbm.1, bf16[1,256,2048]{2,1,0:T(8,128)(2,1)} %k_hbm.1, bf16[1,256,2048]{2,1,0:T(8,128)(2,1)} %v_hbm.1, ...), custom_call_target="tpu_custom_call" | custom-call | tf_op jit(solution)/shard_map/logsparse_backward/pallas_call | solution.py:639
  99.2 3.2 %move_out.1 = (bf16[1,256,2048]{2,1,0:T(8,128)(2,1)}, bf16[1,256,2048]{2,1,0:T(8,128)(2,1)}, bf16[1,256,2048]{2,1,0:T(8,128)(2,1)}, f32[128,2048]{1,0:T(8,128)}) custom-call(bf16[1,256,2048]{2,1,0:T(8,128)(2,1)} %get-tuple-element.8.refs_0_, bf16[1,256,2048]{2,1,0:T(8,128)(2,1)} %get-tuple-element.9.refs_1_, ...), custom_call_target="tpu_custom_call" | custom-call | tf_op jit(solution)/shard_map/move_out/pallas_call | solution.py:623
